TPU v7x, 256 devices: a whole 4x4x8 slice. The times are simulated.
256 devices in a mesh: ctx: 64 (over x, z, y_hi), tp: 4 (over y_lo, core).
Axes of the slice: x: 4, y: 4 (y_hi: 2, y_lo: 2; y = y_hi * 2 + y_lo), z: 8, core: 2. Of those that a mesh axis runs over, the one named last changes fastest.
Arguments:
- trace_q: bfloat16 [8192, 5120], P(('ctx', 'tp')), may hold values from -120 to 120
- trace_key_value: bfloat16 [8192, 2048], P(('ctx', 'tp')), may hold values from -6 to 6
- suffix_q: bfloat16 [64, 128, 5120], P('ctx', 'tp'), may hold values from -120 to 120
- suffix_key_value: bfloat16 [64, 128, 2048], P('ctx', 'tp'), may hold values from -6 to 6
- prefix_len: int32 [64], P('ctx'), may hold values from 2048 to 8192, as said below
- del_start: int32 [64], P('ctx'), may hold values from 0 to 8191, as said below
- del_end: int32 [64], P('ctx'), may hold values from 1 to 8192, as said below
Outputs:
- trace_out: bfloat16 [8192, 5120], P(('ctx', 'tp'))
- suffix_out: bfloat16 [64, 128, 5120], P('ctx', 'tp')
Inputs may be any that keep to these rules, and one draw needn't show every extreme that they name: `prefix_len`: one variant keeps the whole trace as prefix and deletes only its last position. del_start < prefix_len of the same variant. del_start < del_end <= prefix_len of the same variant, and del_end - del_start <= 1024.
All inputs are finite; a program needn't handle non-finite values.
Results may differ from a plain program's by a relative error of at most 0.0075.
Values may be sent and summed in bfloat16 or wider, within the bound.
A program may use at most 192 MiB of HBM per device.

v0:
```python
import math

import jax
import jax.numpy as jnp
from jax import lax
from jax.experimental import pallas as pl
from jax.experimental.pallas import tpu as pltpu
from jax.sharding import PartitionSpec as P

HEAD = 128
GROUP = 5
ROWS = GROUP * 128
QCOL = GROUP * HEAD
SCALE = HEAD ** (-0.5) * math.log2(math.e)
LOW = -1e30
MESH = pl.DeviceIdType.MESH
LAG = 2


def dot(a, b, ca, cb):
    return lax.dot_general(a, b, (((ca,), (cb,)), ((), ())), preferred_element_type=jnp.float32)


def kernel(
    tq, tkv, sq, skv, pre, first, last,
    tout, sout,
    kvb, tqb, sqb, skb, tob, sob, meta_out, meta, acc, m, l,
    st_send, st_recv, meta_send, meta_recv, ag0, ag_send, ag_recv, o_send, o_recv,
):
    ctx = lax.axis_index("ctx")
    tp = lax.axis_index("tp")
    x = ctx // 16
    z = (ctx // 2) % 8
    yh = ctx % 2
    yl = tp // 2
    c = tp % 2
    u = x // 2
    p = ((x + 1) // 2) % 2
    pb = 1 - p
    cb = 1 - c
    head = u * 4 + yh * 2 + yl

    def xof(side, par):
        return par + side * (3 - 2 * par)

    def dev(side, par, zz, yyh, yyl, cc):
        return (xof(side, par) * 16 + zz * 2 + yyh, yyl * 2 + cc)

    def flip(a, by):
        return 1 - a if by else a

    home = (yh + u) % 2
    at_home = c == home
    spot = yl * 2 + c

    up = dev(u, p, (z + 1) % 8, yh, yl, c)
    down = dev(u, p, (z + 7) % 8, yh, yl, c)
    across = dev(u, pb, z, yh, yl, c)
    sibling = dev(u, p, z, yh, yl, cb)

    barrier = pltpu.get_barrier_semaphore()
    for i in range(1, 16):
        pl.semaphore_signal(
            barrier, inc=1, device_id_type=MESH,
            device_id=dev(flip(u, i // 8), p, z, flip(yh, i // 4 % 2), flip(yl, i // 2 % 2), flip(c, i % 2)),
        )
    for d in (up, down, across):
        pl.semaphore_signal(barrier, inc=1, device_id=d, device_id_type=MESH)
    pl.semaphore_wait(barrier, 18)

    def block(par, zz, cc, s):
        xx = par if s == 0 else 3 - par
        return zz * 8 + xx * 2 + (cc + s) % 2

    def rows(b):
        return kvb.at[pl.ds(pl.multiple_of(b * 128, 128), 128), :]

    mine = pl.ds(pl.multiple_of(spot * 32, 32), 32)
    here = pl.ds(pl.multiple_of((z * 8 + x * 2 + yh) * 128 + spot * 32, 32), 32)

    def targets(kind, i):
        h2 = flip(u, i // 4) * 4 + flip(yh, i // 2 % 2) * 2 + flip(yl, i % 2)
        to = dev(flip(u, i // 4), p, z, flip(yh, i // 2 % 2), flip(yl, i % 2), home)
        wide = pl.ds(pl.multiple_of(h2 * QCOL, 128), QCOL)
        pair = pl.ds(pl.multiple_of(h2 * 256, 128), 256)
        src, dst = (
            (tkv.at[:, pair], kvb.at[here, :]),
            (tq.at[:, wide], tqb.at[u, mine, :]),
            (skv.at[:, pair], skb.at[u, mine, :]),
            (sq.at[:, wide], sqb.at[u, mine, :]),
        )[kind]
        remote = pltpu.make_async_remote_copy(
            src, dst, st_send.at[kind, i], st_recv.at[kind, u], device_id=to, device_id_type=MESH
        )
        local = pltpu.make_async_copy(src, dst, st_recv.at[kind, u])
        return remote, local

    def stage_start(kind):
        for i in range(7, -1, -1):
            remote, local = targets(kind, i)
            if i:
                remote.start()
            else:
                pl.when(at_home)(local.start)
                pl.when(jnp.logical_not(at_home))(remote.start)

    def stage_drain(kind):
        for i in range(7, -1, -1):
            remote, _ = targets(kind, i)
            if i:
                remote.wait_send()
            else:
                pl.when(jnp.logical_not(at_home))(remote.wait_send)

    def stage_arrive(kind, s):
        dst = (rows(block(p, z, c, s)), tqb.at[s], skb.at[s], sqb.at[s])[kind]
        pltpu.make_async_copy(dst, dst, st_recv.at[kind, s]).wait()

    def meta_copy(i):
        to = dev(flip(u, i), p, z, yl, c, home)
        is_self = jnp.logical_and(jnp.logical_and(yl == yh, c == yl), at_home) if i == 0 else None
        remote = pltpu.make_async_remote_copy(
            meta_out, meta.at[u], meta_send.at[i], meta_recv.at[u], device_id=to, device_id_type=MESH
        )
        local = pltpu.make_async_copy(meta_out, meta.at[u], meta_recv.at[u])
        return remote, local, is_self

    def pass_on(b, to, sem):
        return pltpu.make_async_remote_copy(rows(b), rows(b), sem, ag_recv.at[b], device_id=to, device_id_type=MESH)

    def arrive(b):
        pltpu.make_async_copy(rows(b), rows(b), ag_recv.at[b]).wait()

    def own_copies():
        a, b = block(p, z, c, 0), block(p, z, c, 1)
        return [
            pass_on(a, across, ag0.at[0]),
            pass_on(a, up, ag0.at[1]),
            pass_on(a, down, ag0.at[2]),
            pass_on(b, up, ag0.at[3]),
            pass_on(b, down, ag0.at[4]),
            pass_on(b, across, ag0.at[5]),
            pass_on(a, sibling, ag0.at[6]),
            pass_on(b, sibling, ag0.at[7]),
        ]

    def near_copies():
        a, b = block(pb, z, c, 0), block(pb, z, c, 1)
        return (
            [pass_on(a, up, ag0.at[8]), pass_on(a, down, ag0.at[9]), pass_on(a, sibling, ag0.at[10])],
            [pass_on(b, sibling, ag0.at[11])],
        )

    def zstep(j):
        return (z + 8 + (1 - 2 * (j % 2)) * ((j + 1) // 2)) % 8

    def ring_copies(j):
        zz = zstep(j)
        step = 2 * (j % 2) - 1
        onward = dev(u, p, (z + 8 + step) % 8, yh, yl, c)
        early = j <= 4
        go = (
            jnp.logical_or(early, j == 5),
            jnp.logical_or(early, j == 6),
            jnp.logical_or(early, j == 5 + c),
        )
        ids = (block(p, zz, c, 0), block(pb, zz, c, 0), block(p, zz, c, 1))
        return zz, go, ids, onward

    def ring(j):
        zz, go, ids, onward = ring_copies(j)
        for i in range(3):
            arrive(ids[i])
            pl.when(go[i])(pass_on(ids[i], onward, ag_send.at[j, i]).start)
            if i == 2:
                pass_on(ids[i], across, ag_send.at[j, 6]).start()
            pass_on(ids[i], sibling, ag_send.at[j, 3 + i]).start()

    def cross(j):
        b = block(pb, zstep(j), c, 1)
        arrive(b)
        pass_on(b, sibling, ag_send.at[j, 7]).start()

    def drain(j):
        zz, go, ids, onward = ring_copies(j)
        for i in range(3):
            pl.when(go[i])(pass_on(ids[i], onward, ag_send.at[j, i]).wait_send)
            pass_on(ids[i], sibling, ag_send.at[j, 3 + i]).wait_send()
        pass_on(ids[2], across, ag_send.at[j, 6]).wait_send()
        pass_on(block(pb, zz, c, 1), sibling, ag_send.at[j, 7]).wait_send()

    def from_sibling(j):
        zz = zstep(j)
        for par in (0, 1):
            for s in (0, 1):
                arrive(block(par, zz, cb, s))

    def queries(buf, s):
        return jnp.concatenate([buf[s, :, i * HEAD:(i + 1) * HEAD] for i in range(GROUP)], axis=0)

    def wide_of(a, n):
        return jnp.concatenate([a] * n, axis=1)

    def fold(q, s, v):
        n = s.shape[1] // 128
        before = m[q]
        top = s[:, :128]
        for t in range(1, n):
            top = jnp.maximum(top, s[:, t * 128:(t + 1) * 128])
        now = jnp.maximum(before, jnp.max(top, axis=1, keepdims=True) * SCALE)
        m[q] = now
        shrink = jnp.exp2(before - now)
        w = jnp.exp2(s * SCALE - wide_of(now, n))
        part = w[:, :128]
        for t in range(1, n):
            part = part + w[:, t * 128:(t + 1) * 128]
        acc[q] = acc[q] * shrink + dot(w.astype(jnp.bfloat16), v, 1, 0)
        l[q] = l[q] * shrink + part

    def trace_body(zz, par, reach):
        at = pl.multiple_of(zz * 1024, 1024)
        counts = [(par if s == 0 else 3 - par) + reach for s in (0, 1)]
        scores = []
        for s in (0, 1):
            n = counts[s]
            if n == 0:
                scores.append(None)
                continue
            sc = dot(queries(tqb, s), kvb[pl.ds(at, n * 256), :HEAD], 1, 1)
            if reach:
                row = lax.broadcasted_iota(jnp.int32, (ROWS, 256), 0) % 128
                lane = lax.broadcasted_iota(jnp.int32, (ROWS, 256), 1)
                seen = lane - row <= (z - zz) * 256 + ((c + s) % 2) * 128
                tail = jnp.where(seen, sc[:, (n - 1) * 256:], LOW)
                sc = tail if n == 1 else jnp.concatenate([sc[:, :(n - 1) * 256], tail], axis=1)
            scores.append(sc)
        for s in (0, 1):
            if scores[s] is not None:
                fold(s, scores[s], kvb[pl.ds(at, counts[s] * 256), HEAD:])

    def trace_step(j):
        zz = zstep(j)
        for par in (0, 1):
            for reach in (0, 1):
                fits = jnp.logical_and(p == par, zz <= z if reach else zz > z)
                pl.when(fits)(lambda par=par, reach=reach: trace_body(zz, par, reach))

    def suffix_self():
        for s in (0, 1):
            sc = dot(queries(sqb, s), skb[s, :, :HEAD], 1, 1)
            row = lax.broadcasted_iota(jnp.int32, (ROWS, 128), 0) % 128
            lane = lax.broadcasted_iota(jnp.int32, (ROWS, 128), 1)
            fold(2 + s, jnp.where(lane <= row, sc, LOW), skb[s, :, HEAD:])

    def suffix_step(j):
        zz = zstep(j)
        at = pl.multiple_of(zz * 1024, 1024)
        scores = []
        for s in (0, 1):
            sc = dot(queries(sqb, s), kvb[pl.ds(at, 1024), :HEAD], 1, 1)
            bias = []
            for t in range(8):
                pos = (t // 2) * 2048 + (t % 2) * 128 + zz * 256 + lax.broadcasted_iota(jnp.int32, (1, 128), 1)
                limit, lo, hi = meta[s, 0:1, :], meta[s, 1:2, :], meta[s, 2:3, :]
                seen = jnp.logical_and(pos < limit, jnp.logical_or(pos < lo, pos >= hi))
                bias.append(jnp.where(seen, 0.0, LOW))
            scores.append(sc + jnp.concatenate(bias, axis=1))
        for s in (0, 1):
            fold(2 + s, scores[s], kvb[pl.ds(at, 1024), HEAD:])

    def returns(kind, s, i):
        buf, out = ((tob, tout), (sob, sout))[kind]
        yyl, cc = flip(yl, i // 2), flip(c, i % 2)
        to = dev(s, p, z, (c + s) % 2, yyl, cc)
        part = pl.ds(pl.multiple_of((yyl * 2 + cc) * 32, 32), 32)
        place = pl.ds(pl.multiple_of(head * QCOL, 128), QCOL)
        remote = pltpu.make_async_remote_copy(
            buf.at[s, part, :], out.at[:, place], o_send.at[kind, s, i], o_recv.at[kind],
            device_id=to, device_id_type=MESH,
        )
        local = pltpu.make_async_copy(buf.at[s, part, :], out.at[:, place], o_recv.at[kind])
        is_self = jnp.logical_and(at_home, u == s) if i == 0 else None
        return remote, local, is_self

    def hand_back(kind):
        buf = (tob, sob)[kind]
        for s in (0, 1):
            q = kind * 2 + s
            res = (acc[q] / jnp.sum(l[q], axis=1, keepdims=True)).astype(jnp.bfloat16)
            for i in range(GROUP):
                buf[s, :, i * HEAD:(i + 1) * HEAD] = res[i * 128:(i + 1) * 128]
            for i in range(3, -1, -1):
                remote, local, is_self = returns(kind, s, i)
                if i:
                    remote.start()
                else:
                    pl.when(is_self)(local.start)
                    pl.when(jnp.logical_not(is_self))(remote.start)

    stage_start(0)
    meta_out[0:1, :] = jnp.full((1, 128), pre[0], jnp.int32)
    meta_out[1:2, :] = jnp.full((1, 128), first[0], jnp.int32)
    meta_out[2:8, :] = jnp.full((6, 128), last[0], jnp.int32)
    stage_start(1)
    for i in (0, 1):
        remote, local, is_self = meta_copy(i)
        if i:
            remote.start()
        else:
            pl.when(is_self)(local.start)
            pl.when(jnp.logical_not(is_self))(remote.start)

    acc[...] = jnp.zeros_like(acc)
    l[...] = jnp.zeros_like(l)
    m[...] = jnp.full_like(m, LOW)

    for s in (0, 1):
        stage_arrive(0, s)
    for copy in own_copies():
        copy.start()
    for s in (0, 1):
        stage_arrive(1, s)
    stage_start(2)
    stage_start(3)
    near_a, near_b = near_copies()
    arrive(block(pb, z, c, 0))
    for copy in near_a:
        copy.start()
    arrive(block(pb, z, c, 1))
    for copy in near_b:
        copy.start()
    ring(1)

    def step(k, _):
        @pl.when(k < 8)
        def _():
            from_sibling(k)
            trace_step(k)

        pl.when(k < 6)(lambda: ring(k + 2))
        pl.when(k < 7)(lambda: cross(k + 1))

        pl.when(k == 7)(lambda: hand_back(0))

        @pl.when(k == LAG - 1)
        def _():
            for s in (0, 1):
                stage_arrive(2, s)
                stage_arrive(3, s)
                pltpu.make_async_copy(meta.at[s], meta.at[s], meta_recv.at[s]).wait()
            suffix_self()

        pl.when(k >= LAG)(lambda: suffix_step(k - LAG))
        return 0

    lax.fori_loop(0, 8 + LAG, step, 0)
    hand_back(1)

    for kind in range(4):
        stage_drain(kind)
    for i in (0, 1):
        remote, _, is_self = meta_copy(i)
        if i:
            remote.wait_send()
        else:
            pl.when(jnp.logical_not(is_self))(remote.wait_send)
    for copy in own_copies() + near_a + near_b:
        copy.wait_send()

    def finish(j, _):
        drain(j)
        return 0

    lax.fori_loop(1, 8, finish, 0)
    for kind in (0, 1):
        for s in (0, 1):
            for i in range(4):
                remote, _, is_self = returns(kind, s, i)
                if i:
                    remote.wait_send()
                else:
                    pl.when(jnp.logical_not(is_self))(remote.wait_send)
    pltpu.make_async_copy(tout, tout, o_recv.at[0]).wait()
    pltpu.make_async_copy(sout, sout, o_recv.at[1]).wait()


def local(trace_q, trace_key_value, suffix_q, suffix_key_value, prefix_len, del_start, del_end):
    any_space = pl.BlockSpec(memory_space=pl.ANY)
    scalar = pl.BlockSpec(memory_space=pltpu.SMEM)
    bf16, f32 = jnp.bfloat16, jnp.float32
    tout, sout = pl.pallas_call(
        kernel,
        out_shape=(
            jax.ShapeDtypeStruct(trace_q.shape, bf16),
            jax.ShapeDtypeStruct(trace_q.shape, bf16),
        ),
        in_specs=[any_space] * 4 + [scalar] * 3,
        out_specs=(any_space, any_space),
        scratch_shapes=[
            pltpu.VMEM((8192, 256), bf16),
            pltpu.VMEM((2, 128, QCOL), bf16),
            pltpu.VMEM((2, 128, QCOL), bf16),
            pltpu.VMEM((2, 128, 256), bf16),
            pltpu.VMEM((2, 128, QCOL), bf16),
            pltpu.VMEM((2, 128, QCOL), bf16),
            pltpu.VMEM((8, 128), jnp.int32),
            pltpu.VMEM((2, 8, 128), jnp.int32),
            pltpu.VMEM((4, ROWS, HEAD), f32),
            pltpu.VMEM((4, ROWS, HEAD), f32),
            pltpu.VMEM((4, ROWS, HEAD), f32),
            pltpu.SemaphoreType.DMA((4, 8)),
            pltpu.SemaphoreType.DMA((4, 2)),
            pltpu.SemaphoreType.DMA((2,)),
            pltpu.SemaphoreType.DMA((2,)),
            pltpu.SemaphoreType.DMA((12,)),
            pltpu.SemaphoreType.DMA((8, 8)),
            pltpu.SemaphoreType.DMA((64,)),
            pltpu.SemaphoreType.DMA((2, 2, 4)),
            pltpu.SemaphoreType.DMA((2,)),
        ],
        compiler_params=pltpu.CompilerParams(
            collective_id=0, has_side_effects=True, vmem_limit_bytes=56 * 2**20
        ),
        cost_estimate=pl.CostEstimate(flops=9 * 10**9, bytes_accessed=4 * 10**6, transcendentals=17 * 10**6),
    )(
        trace_q, trace_key_value, suffix_q[0], suffix_key_value[0], prefix_len, del_start, del_end
    )
    return tout, sout[None]


def solution(mesh):
    return jax.shard_map(
        local,
        mesh=mesh,
        in_specs=(
            P(("ctx", "tp"), None),
            P(("ctx", "tp"), None),
            P("ctx", "tp", None),
            P("ctx", "tp", None),
            P("ctx"),
            P("ctx"),
            P("ctx"),
        ),
        out_specs=(P(("ctx", "tp"), None), P("ctx", "tp", None)),
        check_vma=False,
    )
```

profile of v0, /device:TPU:1, one launch (start us, length us, event | category | flops | bytes accessed | tf_op | source)
XLA Modules:
  0.0 68.0 jit_solution(6670117737594532220)
XLA Ops:
  2.6 62.9 %shard_map.86 = (bf16[32,5120]{1,0:T(8,128)(2,1)}, bf16[32,5120]{1,0:T(8,128)(2,1)}) custom-call(bf16[32,5120]{1,0:T(8,128)(2,1)} %tq.1, bf16[32,2048]{1,0:T(8,128)(2,1)} %tkv.1, bf16[32,5120]{1,0:T(8,128)(2,1)} %bitcast.4, bf16[32,2048]{1,0:T(8,128)(2,1)} %bitcast.5, s32[1]{0:T(128)S(6)} %copy.11.pre, s32[1]{0:T(128)S(6)} %copy.12.first, s32[1]{0:T(128)S(6)} %copy.13.last), custom_call_target="tpu_custom_call" | custom-call | flops 8999999488 | bytes 4000000 | tf_op jit(solution)/shard_map/pallas_call | solution.py:391
  65.5 0.0 copy-start
  65.5 1.8 %copy.14 = bf16[32,5120]{1,0:T(8,128)(2,1)} copy(bf16[32,5120]{1,0:T(8,128)(2,1)} %get-tuple-element.8) | data formatting | bytes 655360
  67.3 0.0 copy-done
  67.3 0.7 %copy.15 = bf16[1,32,5120]{2,1,0:T(8,128)(2,1)} copy(bf16[1,32,5120]{2,1,0:T(8,128)(2,1)S(1)} %bitcast.3) | data formatting | bytes 655360
Async XLA Ops:
  65.5 1.8 %copy-start = (bf16[32,5120]{1,0:T(8,128)(2,1)S(1)}, bf16[32,5120]{1,0:T(8,128)(2,1)}, u32[]{:S(2)}) copy-start(bf16[32,5120]{1,0:T(8,128)(2,1)} %get-tuple-element.5) | copy-start | bytes 983044
where the time goes:
time: 68.1 us; the launch traced here: 68 us
  Pallas kernels  62.9 us (92%)
  between operations  2.58 us (4%)
  local copies, waits for them, and re-layouts  2.49 us (4%)
    pallas_call x1, Pallas kernels, local(): pl.pallas_call(kernel, out_shape=(jax.ShapeDtypeStruct(trace_q.shape, bf1...  62.9 us
    unnamed x4, local copies, waits for them, and re-layouts  2.49 us

commit v1 on v0

--- a/solution.py
+++ b/solution.py
@@ -14,7 +14,6 @@
 SCALE = HEAD ** (-0.5) * math.log2(math.e)
 LOW = -1e30
 MESH = pl.DeviceIdType.MESH
-LAG = 2
 
 
 def dot(a, b, ca, cb):
@@ -59,14 +58,16 @@
     sibling = dev(u, p, z, yh, yl, cb)
 
     barrier = pltpu.get_barrier_semaphore()
-    for i in range(1, 16):
+    for i in range(1, 32):
         pl.semaphore_signal(
             barrier, inc=1, device_id_type=MESH,
-            device_id=dev(flip(u, i // 8), p, z, flip(yh, i // 4 % 2), flip(yl, i // 2 % 2), flip(c, i % 2)),
-        )
-    for d in (up, down, across):
+            device_id=dev(
+                flip(u, i // 8 % 2), flip(p, i // 16), z, flip(yh, i // 4 % 2), flip(yl, i // 2 % 2), flip(c, i % 2)
+            ),
+        )
+    for d in (up, down):
         pl.semaphore_signal(barrier, inc=1, device_id=d, device_id_type=MESH)
-    pl.semaphore_wait(barrier, 18)
+    pl.semaphore_wait(barrier, 33)
 
     def block(par, zz, cc, s):
         xx = par if s == 0 else 3 - par
@@ -80,7 +81,7 @@
 
     def targets(kind, i):
         h2 = flip(u, i // 4) * 4 + flip(yh, i // 2 % 2) * 2 + flip(yl, i % 2)
-        to = dev(flip(u, i // 4), p, z, flip(yh, i // 2 % 2), flip(yl, i % 2), home)
+        to = dev(flip(u, i // 4), pb if kind == 4 else p, z, flip(yh, i // 2 % 2), flip(yl, i % 2), home)
         wide = pl.ds(pl.multiple_of(h2 * QCOL, 128), QCOL)
         pair = pl.ds(pl.multiple_of(h2 * 256, 128), 256)
         src, dst = (
@@ -88,6 +89,7 @@
             (tq.at[:, wide], tqb.at[u, mine, :]),
             (skv.at[:, pair], skb.at[u, mine, :]),
             (sq.at[:, wide], sqb.at[u, mine, :]),
+            (tkv.at[:, pair], kvb.at[here, :]),
         )[kind]
         remote = pltpu.make_async_remote_copy(
             src, dst, st_send.at[kind, i], st_recv.at[kind, u], device_id=to, device_id_type=MESH
@@ -98,7 +100,7 @@
     def stage_start(kind):
         for i in range(7, -1, -1):
             remote, local = targets(kind, i)
-            if i:
+            if i or kind == 4:
                 remote.start()
             else:
                 pl.when(at_home)(local.start)
@@ -107,13 +109,13 @@
     def stage_drain(kind):
         for i in range(7, -1, -1):
             remote, _ = targets(kind, i)
-            if i:
+            if i or kind == 4:
                 remote.wait_send()
             else:
                 pl.when(jnp.logical_not(at_home))(remote.wait_send)
 
     def stage_arrive(kind, s):
-        dst = (rows(block(p, z, c, s)), tqb.at[s], skb.at[s], sqb.at[s])[kind]
+        dst = (rows(block(p, z, c, s)), tqb.at[s], skb.at[s], sqb.at[s], rows(block(pb, z, c, s)))[kind]
         pltpu.make_async_copy(dst, dst, st_recv.at[kind, s]).wait()
 
     def meta_copy(i):
@@ -134,21 +136,20 @@
     def own_copies():
         a, b = block(p, z, c, 0), block(p, z, c, 1)
         return [
-            pass_on(a, across, ag0.at[0]),
-            pass_on(a, up, ag0.at[1]),
-            pass_on(a, down, ag0.at[2]),
-            pass_on(b, up, ag0.at[3]),
-            pass_on(b, down, ag0.at[4]),
-            pass_on(b, across, ag0.at[5]),
+            pass_on(b, up, ag0.at[0]),
+            pass_on(b, down, ag0.at[1]),
+            pass_on(b, across, ag0.at[2]),
+            pass_on(a, up, ag0.at[3]),
+            pass_on(a, down, ag0.at[4]),
+            pass_on(b, sibling, ag0.at[5]),
             pass_on(a, sibling, ag0.at[6]),
-            pass_on(b, sibling, ag0.at[7]),
         ]
 
     def near_copies():
         a, b = block(pb, z, c, 0), block(pb, z, c, 1)
         return (
-            [pass_on(a, up, ag0.at[8]), pass_on(a, down, ag0.at[9]), pass_on(a, sibling, ag0.at[10])],
-            [pass_on(b, sibling, ag0.at[11])],
+            [pass_on(a, up, ag0.at[7]), pass_on(a, down, ag0.at[8]), pass_on(a, sibling, ag0.at[9])],
+            [pass_on(b, sibling, ag0.at[10])],
         )
 
     def zstep(j):
@@ -167,9 +168,9 @@
         ids = (block(p, zz, c, 0), block(pb, zz, c, 0), block(p, zz, c, 1))
         return zz, go, ids, onward
 
-    def ring(j):
+    def ring(j, which):
         zz, go, ids, onward = ring_copies(j)
-        for i in range(3):
+        for i in which:
             arrive(ids[i])
             pl.when(go[i])(pass_on(ids[i], onward, ag_send.at[j, i]).start)
             if i == 2:
@@ -201,21 +202,24 @@
     def wide_of(a, n):
         return jnp.concatenate([a] * n, axis=1)
 
-    def fold(q, s, v):
-        n = s.shape[1] // 128
-        before = m[q]
-        top = s[:, :128]
-        for t in range(1, n):
-            top = jnp.maximum(top, s[:, t * 128:(t + 1) * 128])
+    def fold(q, pieces, r=slice(0, ROWS)):
+        before = m[q, r]
+        cols = [sc[:, t * 128:(t + 1) * 128] for sc, _ in pieces for t in range(sc.shape[1] // 128)]
+        top = cols[0]
+        for col in cols[1:]:
+            top = jnp.maximum(top, col)
         now = jnp.maximum(before, jnp.max(top, axis=1, keepdims=True) * SCALE)
-        m[q] = now
+        m[q, r] = now
         shrink = jnp.exp2(before - now)
-        w = jnp.exp2(s * SCALE - wide_of(now, n))
-        part = w[:, :128]
-        for t in range(1, n):
-            part = part + w[:, t * 128:(t + 1) * 128]
-        acc[q] = acc[q] * shrink + dot(w.astype(jnp.bfloat16), v, 1, 0)
-        l[q] = l[q] * shrink + part
+        total, part = acc[q, r] * shrink, l[q, r] * shrink
+        for sc, v in pieces:
+            n = sc.shape[1] // 128
+            w = jnp.exp2(sc * SCALE - wide_of(now, n))
+            for t in range(n):
+                part = part + w[:, t * 128:(t + 1) * 128]
+            total = total + dot(w.astype(jnp.bfloat16), v, 1, 0)
+        acc[q, r] = total
+        l[q, r] = part
 
     def trace_body(zz, par, reach):
         at = pl.multiple_of(zz * 1024, 1024)
@@ -236,7 +240,7 @@
             scores.append(sc)
         for s in (0, 1):
             if scores[s] is not None:
-                fold(s, scores[s], kvb[pl.ds(at, counts[s] * 256), HEAD:])
+                fold(s, [(scores[s], kvb[pl.ds(at, counts[s] * 256), HEAD:])])
 
     def trace_step(j):
         zz = zstep(j)
@@ -250,23 +254,26 @@
             sc = dot(queries(sqb, s), skb[s, :, :HEAD], 1, 1)
             row = lax.broadcasted_iota(jnp.int32, (ROWS, 128), 0) % 128
             lane = lax.broadcasted_iota(jnp.int32, (ROWS, 128), 1)
-            fold(2 + s, jnp.where(lane <= row, sc, LOW), skb[s, :, HEAD:])
-
-    def suffix_step(j):
-        zz = zstep(j)
-        at = pl.multiple_of(zz * 1024, 1024)
-        scores = []
-        for s in (0, 1):
-            sc = dot(queries(sqb, s), kvb[pl.ds(at, 1024), :HEAD], 1, 1)
+            fold(2 + s, [(jnp.where(lane <= row, sc, LOW), skb[s, :, HEAD:])])
+
+    def suffix_step(s, planes):
+        q = queries(sqb, s)
+        limit, lo, hi = meta[s, 0:1, :], meta[s, 1:2, :], meta[s, 2:3, :]
+        biases = []
+        for zz in planes:
             bias = []
             for t in range(8):
                 pos = (t // 2) * 2048 + (t % 2) * 128 + zz * 256 + lax.broadcasted_iota(jnp.int32, (1, 128), 1)
-                limit, lo, hi = meta[s, 0:1, :], meta[s, 1:2, :], meta[s, 2:3, :]
                 seen = jnp.logical_and(pos < limit, jnp.logical_or(pos < lo, pos >= hi))
                 bias.append(jnp.where(seen, 0.0, LOW))
-            scores.append(sc + jnp.concatenate(bias, axis=1))
-        for s in (0, 1):
-            fold(2 + s, scores[s], kvb[pl.ds(at, 1024), HEAD:])
+            biases.append(jnp.concatenate(bias, axis=1))
+        halves = (slice(0, ROWS // 2), slice(ROWS // 2, ROWS))
+        places = [pl.ds(pl.multiple_of(zz * 1024, 1024), 1024) for zz in planes]
+        scores = [
+            [dot(q[r], kvb[at, :HEAD], 1, 1) + bias for at, bias in zip(places, biases)] for r in halves
+        ]
+        for r, row in zip(halves, scores):
+            fold(2 + s, [(sc, kvb[at, HEAD:]) for sc, at in zip(row, places)], r)
 
     def returns(kind, s, i):
         buf, out = ((tob, tout), (sob, sout))[kind]
@@ -282,9 +289,9 @@
         is_self = jnp.logical_and(at_home, u == s) if i == 0 else None
         return remote, local, is_self
 
-    def hand_back(kind):
+    def hand_back(kind, slots):
         buf = (tob, sob)[kind]
-        for s in (0, 1):
+        for s in slots:
             q = kind * 2 + s
             res = (acc[q] / jnp.sum(l[q], axis=1, keepdims=True)).astype(jnp.bfloat16)
             for i in range(GROUP):
@@ -298,6 +305,7 @@
                     pl.when(jnp.logical_not(is_self))(remote.start)
 
     stage_start(0)
+    pl.when(u == 0)(lambda: stage_start(4))
     meta_out[0:1, :] = jnp.full((1, 128), pre[0], jnp.int32)
     meta_out[1:2, :] = jnp.full((1, 128), first[0], jnp.int32)
     meta_out[2:8, :] = jnp.full((6, 128), last[0], jnp.int32)
@@ -318,31 +326,29 @@
         stage_arrive(0, s)
     for copy in own_copies():
         copy.start()
-    for s in (0, 1):
-        stage_arrive(1, s)
+    stage_start(3)
     stage_start(2)
-    stage_start(3)
     near_a, near_b = near_copies()
-    arrive(block(pb, z, c, 0))
+    stage_arrive(4, 0)
     for copy in near_a:
         copy.start()
     arrive(block(pb, z, c, 1))
     for copy in near_b:
         copy.start()
-    ring(1)
-
-    def step(k, _):
-        @pl.when(k < 8)
-        def _():
-            from_sibling(k)
-            trace_step(k)
-
-        pl.when(k < 6)(lambda: ring(k + 2))
-        pl.when(k < 7)(lambda: cross(k + 1))
-
-        pl.when(k == 7)(lambda: hand_back(0))
-
-        @pl.when(k == LAG - 1)
+    for s in (0, 1):
+        stage_arrive(1, s)
+
+    def plane(j):
+        from_sibling(j)
+        trace_step(j)
+
+    def step(g, _):
+        pl.when(g <= 3)(lambda: ring(2 * g + 1, (2,)))
+        pl.when(g <= 2)(lambda: ring(2 * g + 2, (2,)))
+        pl.when(jnp.logical_and(g >= 1, g <= 4))(lambda: plane(2 * g - 1))
+        pl.when(g == 4)(lambda: hand_back(0, (0, 1)))
+
+        @pl.when(g == 1)
         def _():
             for s in (0, 1):
                 stage_arrive(2, s)
@@ -350,14 +356,22 @@
                 pltpu.make_async_copy(meta.at[s], meta.at[s], meta_recv.at[s]).wait()
             suffix_self()
 
-        pl.when(k >= LAG)(lambda: suffix_step(k - LAG))
+        pl.when(jnp.logical_and(g >= 1, g <= 4))(lambda: suffix_step(0, (zstep(2 * g - 2), zstep(2 * g - 1))))
+        pl.when(g == 4)(lambda: hand_back(1, (0,)))
+        pl.when(g <= 3)(lambda: ring(2 * g + 1, (0, 1)))
+        pl.when(g <= 2)(lambda: ring(2 * g + 2, (0, 1)))
+        pl.when(g <= 3)(lambda: plane(2 * g))
+        pl.when(g <= 3)(lambda: cross(2 * g + 1))
+        pl.when(g <= 2)(lambda: cross(2 * g + 2))
+        pl.when(g >= 2)(lambda: suffix_step(1, (zstep(2 * g - 4), zstep(2 * g - 3))))
         return 0
 
-    lax.fori_loop(0, 8 + LAG, step, 0)
-    hand_back(1)
+    lax.fori_loop(0, 6, step, 0)
+    hand_back(1, (1,))
 
     for kind in range(4):
         stage_drain(kind)
+    pl.when(u == 0)(lambda: stage_drain(4))
     for i in (0, 1):
         remote, _, is_self = meta_copy(i)
         if i:
@@ -382,6 +396,11 @@
                     pl.when(jnp.logical_not(is_self))(remote.wait_send)
     pltpu.make_async_copy(tout, tout, o_recv.at[0]).wait()
     pltpu.make_async_copy(sout, sout, o_recv.at[1]).wait()
+
+
+def settle(a, b, a_out, b_out):
+    a_out[...] = a[...]
+    b_out[...] = b[...]
 
 
 def local(trace_q, trace_key_value, suffix_q, suffix_key_value, prefix_len, del_start, del_end):
@@ -408,11 +427,11 @@
             pltpu.VMEM((4, ROWS, HEAD), f32),
             pltpu.VMEM((4, ROWS, HEAD), f32),
             pltpu.VMEM((4, ROWS, HEAD), f32),
-            pltpu.SemaphoreType.DMA((4, 8)),
-            pltpu.SemaphoreType.DMA((4, 2)),
+            pltpu.SemaphoreType.DMA((5, 8)),
+            pltpu.SemaphoreType.DMA((5, 2)),
             pltpu.SemaphoreType.DMA((2,)),
             pltpu.SemaphoreType.DMA((2,)),
-            pltpu.SemaphoreType.DMA((12,)),
+            pltpu.SemaphoreType.DMA((11,)),
             pltpu.SemaphoreType.DMA((8, 8)),
             pltpu.SemaphoreType.DMA((64,)),
             pltpu.SemaphoreType.DMA((2, 2, 4)),
@@ -425,6 +444,13 @@
     )(
         trace_q, trace_key_value, suffix_q[0], suffix_key_value[0], prefix_len, del_start, del_end
     )
+    whole = pl.BlockSpec(memory_space=pltpu.VMEM)
+    tout, sout = pl.pallas_call(
+        settle,
+        out_shape=(jax.ShapeDtypeStruct(trace_q.shape, bf16),) * 2,
+        in_specs=[whole] * 2,
+        out_specs=(whole, whole),
+    )(tout, sout)
     return tout, sout[None]
 
 

time: 68.1 us -> 64.1 us (0.941); the launches traced: 68 us -> 63.3 us
  local copies, waits for them, and re-layouts: 2.49 us -> 0 us
  Pallas kernels: 62.9 us -> 60.7 us
    pallas_call x1, Pallas kernels: 62.9 us -> 58.8 us  [local(): pl.pallas_call(kernel, out_shape=(jax.ShapeDtypeStruct(trace_q.shape, bf1...]
    unnamed x4 -> x0, local copies, waits for them, and re-layouts: 2.49 us -> none
    pallas_call x0 -> x1, Pallas kernels: none -> 1.93 us  [local(): pl.pallas_call(settle, out_shape=(jax.ShapeDtypeStruct(trace_q.shape, bf1...]
where the time goes in v1:
time: 64.1 us; the launch traced here: 63.3 us
  Pallas kernels  60.7 us (95%)
  between operations  2.58 us (4%)
    pallas_call x1, Pallas kernels, local(): pl.pallas_call(kernel, out_shape=(jax.ShapeDtypeStruct(trace_q.shape, bf1...  58.8 us
    pallas_call x1, Pallas kernels, local(): pl.pallas_call(settle, out_shape=(jax.ShapeDtypeStruct(trace_q.shape, bf1...  1.93 us

profile of v1, /device:TPU:1, one launch (start us, length us, event | category | flops | bytes accessed | tf_op | source)
XLA Modules:
  0.0 63.3 jit_solution(10894928862241200192)
XLA Ops:
  2.6 58.8 %shard_map.86 = (bf16[32,5120]{1,0:T(8,128)(2,1)}, bf16[32,5120]{1,0:T(8,128)(2,1)}) custom-call(bf16[32,5120]{1,0:T(8,128)(2,1)} %tq.1, bf16[32,2048]{1,0:T(8,128)(2,1)} %tkv.1, bf16[32,5120]{1,0:T(8,128)(2,1)} %bitcast.3, bf16[32,2048]{1,0:T(8,128)(2,1)} %bitcast.5, s32[1]{0:T(128)S(6)} %copy.9.pre, s32[1]{0:T(128)S(6)} %copy.10.first, s32[1]{0:T(128)S(6)} %copy.11.last), custom_call_target="tpu_custom_call" | custom-call | flops 8999999488 | bytes 4000000 | tf_op jit(solution)/shard_map/pallas_call | solution.py:410
  61.4 1.9 %shard_map.87 = (bf16[32,5120]{1,0:T(8,128)(2,1)}, bf16[32,5120]{1,0:T(8,128)(2,1)}) custom-call(bf16[32,5120]{1,0:T(8,128)(2,1)} %get-tuple-element.6.a, bf16[32,5120]{1,0:T(8,128)(2,1)} %get-tuple-element.7.b), custom_call_target="tpu_custom_call" | custom-call | tf_op jit(solution)/shard_map/pallas_call | solution.py:448

commit v2 on v1

--- a/solution.py
+++ b/solution.py
@@ -223,24 +223,24 @@
 
     def trace_body(zz, par, reach):
         at = pl.multiple_of(zz * 1024, 1024)
-        counts = [(par if s == 0 else 3 - par) + reach for s in (0, 1)]
-        scores = []
+        half = ROWS // 2
+        work = []
         for s in (0, 1):
-            n = counts[s]
+            n = (par if s == 0 else 3 - par) + reach
             if n == 0:
-                scores.append(None)
                 continue
-            sc = dot(queries(tqb, s), kvb[pl.ds(at, n * 256), :HEAD], 1, 1)
-            if reach:
-                row = lax.broadcasted_iota(jnp.int32, (ROWS, 256), 0) % 128
-                lane = lax.broadcasted_iota(jnp.int32, (ROWS, 256), 1)
-                seen = lane - row <= (z - zz) * 256 + ((c + s) % 2) * 128
-                tail = jnp.where(seen, sc[:, (n - 1) * 256:], LOW)
-                sc = tail if n == 1 else jnp.concatenate([sc[:, :(n - 1) * 256], tail], axis=1)
-            scores.append(sc)
-        for s in (0, 1):
-            if scores[s] is not None:
-                fold(s, [(scores[s], kvb[pl.ds(at, counts[s] * 256), HEAD:])])
+            q = queries(tqb, s)
+            for r in (slice(0, half), slice(half, ROWS)):
+                sc = dot(q[r], kvb[pl.ds(at, n * 256), :HEAD], 1, 1)
+                if reach:
+                    row = (lax.broadcasted_iota(jnp.int32, (half, 256), 0) + r.start) % 128
+                    lane = lax.broadcasted_iota(jnp.int32, (half, 256), 1)
+                    seen = lane - row <= (z - zz) * 256 + ((c + s) % 2) * 128
+                    tail = jnp.where(seen, sc[:, (n - 1) * 256:], LOW)
+                    sc = tail if n == 1 else jnp.concatenate([sc[:, :(n - 1) * 256], tail], axis=1)
+                work.append((s, sc, n, r))
+        for s, sc, n, r in work:
+            fold(s, [(sc, kvb[pl.ds(at, n * 256), HEAD:])], r)
 
     def trace_step(j):
         zz = zstep(j)
@@ -345,8 +345,11 @@
     def step(g, _):
         pl.when(g <= 3)(lambda: ring(2 * g + 1, (2,)))
         pl.when(g <= 2)(lambda: ring(2 * g + 2, (2,)))
-        pl.when(jnp.logical_and(g >= 1, g <= 4))(lambda: plane(2 * g - 1))
+        pl.when(g <= 4)(lambda: plane(jnp.maximum(2 * g - 1, 0)))
         pl.when(g == 4)(lambda: hand_back(0, (0, 1)))
+
+        pl.when(g <= 3)(lambda: ring(2 * g + 1, (0,)))
+        pl.when(g <= 2)(lambda: ring(2 * g + 2, (0,)))
 
         @pl.when(g == 1)
         def _():
@@ -358,15 +361,15 @@
 
         pl.when(jnp.logical_and(g >= 1, g <= 4))(lambda: suffix_step(0, (zstep(2 * g - 2), zstep(2 * g - 1))))
         pl.when(g == 4)(lambda: hand_back(1, (0,)))
-        pl.when(g <= 3)(lambda: ring(2 * g + 1, (0, 1)))
-        pl.when(g <= 2)(lambda: ring(2 * g + 2, (0, 1)))
-        pl.when(g <= 3)(lambda: plane(2 * g))
+        pl.when(g <= 3)(lambda: ring(2 * g + 1, (1,)))
+        pl.when(g <= 2)(lambda: ring(2 * g + 2, (1,)))
+        pl.when(jnp.logical_and(g >= 1, g <= 3))(lambda: plane(2 * g))
         pl.when(g <= 3)(lambda: cross(2 * g + 1))
         pl.when(g <= 2)(lambda: cross(2 * g + 2))
-        pl.when(g >= 2)(lambda: suffix_step(1, (zstep(2 * g - 4), zstep(2 * g - 3))))
+        pl.when(g >= 1)(lambda: suffix_step(1, (zstep(2 * g - 2), zstep(2 * g - 1))))
         return 0
 
-    lax.fori_loop(0, 6, step, 0)
+    lax.fori_loop(0, 5, step, 0)
     hand_back(1, (1,))
 
     for kind in range(4):
@@ -398,9 +401,17 @@
     pltpu.make_async_copy(sout, sout, o_recv.at[1]).wait()
 
 
-def settle(a, b, a_out, b_out):
-    a_out[...] = a[...]
-    b_out[...] = b[...]
+def settle(a, b, a_out, b_out, a_here, b_here, sems):
+    pairs = ((a, a_here, a_out), (b, b_here, b_out))
+    reads = [pltpu.make_async_copy(src, via, sems.at[i]) for i, (src, via, _) in enumerate(pairs)]
+    writes = [pltpu.make_async_copy(via, dst, sems.at[2 + i]) for i, (_, via, dst) in enumerate(pairs)]
+    for copy in reads:
+        copy.start()
+    for read, write in zip(reads, writes):
+        read.wait()
+        write.start()
+    for copy in writes:
+        copy.wait()
 
 
 def local(trace_q, trace_key_value, suffix_q, suffix_key_value, prefix_len, del_start, del_end):
@@ -444,12 +455,12 @@
     )(
         trace_q, trace_key_value, suffix_q[0], suffix_key_value[0], prefix_len, del_start, del_end
     )
-    whole = pl.BlockSpec(memory_space=pltpu.VMEM)
     tout, sout = pl.pallas_call(
         settle,
         out_shape=(jax.ShapeDtypeStruct(trace_q.shape, bf16),) * 2,
-        in_specs=[whole] * 2,
-        out_specs=(whole, whole),
+        in_specs=[any_space] * 2,
+        out_specs=(any_space, any_space),
+        scratch_shapes=[pltpu.VMEM(trace_q.shape, bf16)] * 2 + [pltpu.SemaphoreType.DMA((4,))],
     )(tout, sout)
     return tout, sout[None]
 

time: 64.1 us -> 64 us (level); the launches traced: 63.3 us -> 63.9 us
  no operation moved by 1% of the time
where the time goes in v2:
time: 64 us; the launch traced here: 63.9 us
  Pallas kernels  61.3 us (96%)
  between operations  2.58 us (4%)
    pallas_call x1, Pallas kernels, local(): pl.pallas_call(kernel, out_shape=(jax.ShapeDtypeStruct(trace_q.shape, bf1...  59.4 us
    pallas_call x1, Pallas kernels, local(): pl.pallas_call(settle, out_shape=(jax.ShapeDtypeStruct(trace_q.shape, bf1...  1.84 us

profile of v2, /device:TPU:1, one launch (start us, length us, event | category | flops | bytes accessed | tf_op | source)
XLA Modules:
  0.0 63.9 jit_solution(16872895306126983147)
XLA Ops:
  2.6 59.4 %shard_map.86 = (bf16[32,5120]{1,0:T(8,128)(2,1)}, bf16[32,5120]{1,0:T(8,128)(2,1)}) custom-call(bf16[32,5120]{1,0:T(8,128)(2,1)} %tq.1, bf16[32,2048]{1,0:T(8,128)(2,1)} %tkv.1, bf16[32,5120]{1,0:T(8,128)(2,1)} %bitcast.3, bf16[32,2048]{1,0:T(8,128)(2,1)} %bitcast.5, s32[1]{0:T(128)S(6)} %copy.9.pre, s32[1]{0:T(128)S(6)} %copy.10.first, s32[1]{0:T(128)S(6)} %copy.11.last), custom_call_target="tpu_custom_call" | custom-call | flops 8999999488 | bytes 4000000 | tf_op jit(solution)/shard_map/pallas_call | solution.py:421
  62.0 1.8 %shard_map.87 = (bf16[32,5120]{1,0:T(8,128)(2,1)}, bf16[32,5120]{1,0:T(8,128)(2,1)}) custom-call(bf16[32,5120]{1,0:T(8,128)(2,1)} %get-tuple-element.6.a, bf16[32,5120]{1,0:T(8,128)(2,1)} %get-tuple-element.7.b), custom_call_target="tpu_custom_call" | custom-call | tf_op jit(solution)/shard_map/pallas_call | solution.py:458
